TPU v7x, 256 devices: a whole 4x4x8 slice. The times are simulated.
256 devices in a mesh: tm: 128 (over y, x_lo, z, core), mp: 2 (over x_hi).
Axes of the slice: x: 4 (x_hi: 2, x_lo: 2; x = x_hi * 2 + x_lo), y: 4, z: 8, core: 2. Of those that a mesh axis runs over, the one named last changes fastest.
Arguments:
- global_q: bfloat16 [4096, 2048], P('tm', 'mp'), may hold values from -9 to 9
- global_k: bfloat16 [4096, 2048], P('tm', 'mp'), may hold values from -7 to 7
- global_v: bfloat16 [4096, 2048], P('tm', 'mp'), may hold values from -6 to 6
- keyframe_mask: int32 [128], P('tm'), may hold values 0 or 1
- global_wo: bfloat16 [2048, 2048], P('mp'), may hold values from -0.125 to 0.125
- local_q: bfloat16 [123904, 2048], P('tm', 'mp'), may hold values from -9 to 9, as said below
- local_k: bfloat16 [123904, 2048], P('tm', 'mp'), may hold values from -7 to 7, as said below
- local_v: bfloat16 [123904, 2048], P('tm', 'mp'), may hold values from -6 to 6
- anchor_k: bfloat16 [11264, 2048], P('tm', 'mp'), may hold values from -7 to 7
- anchor_v: bfloat16 [11264, 2048], P('tm', 'mp'), may hold values from -6 to 6
Outputs:
- global_out: bfloat16 [4096, 2048], P('tm', 'mp')
- local_out: bfloat16 [123904, 2048], P('tm', 'mp')
Inputs may be any that keep to these rules, and one draw needn't show every extreme that they name: `local_q`: entries of the generated frames' queries. `local_k`: entries of the generated frames' keys.
All inputs are finite; a program needn't handle non-finite values. No bound on the sum of `keyframe_mask` on one device may be relied on, other than what follows from the above.
Results may differ from a plain program's by a relative error of at most 0.014.
Values may be sent and summed in bfloat16 or wider, within the bound.
A program may use at most 128 MiB of HBM per device.

v0:
```python
import math

import jax
import jax.numpy as jnp
from jax import lax
from jax.sharding import PartitionSpec as P

HD = 128
PG = 32


neg_fill = -1e30


def passed_along(block, axis, distance):
    devices = range(lax.axis_size(axis))
    route = [(i - distance, i) for i in devices if i - distance in devices]
    return lax.ppermute(block, axis, route)


def head_major(rows):
    return jnp.transpose(rows.reshape(rows.shape[0], -1, HD), (1, 0, 2))


def softmax_parts(q_heads, k_heads, v_heads, valid):
    factor = 1.0 / math.sqrt(HD)

    def one_head(operands):
        q_one, k_one, v_one = operands
        scores = jnp.einsum("qd,kd->qk", q_one, k_one, preferred_element_type=jnp.float32) * factor
        scores = jnp.where(valid[None, :], scores, neg_fill)
        peak = jnp.max(scores, axis=1)
        weights = jnp.where(valid[None, :], jnp.exp(scores - peak[:, None]), 0.0)
        summed = jnp.dot(weights.astype(jnp.bfloat16), v_one, preferred_element_type=jnp.float32)
        return (peak, jnp.sum(weights, axis=1), summed)

    return lax.map(one_head, (q_heads, k_heads, v_heads))


def keyframe_step(carry, k_rows, v_rows, key_given, q_heads, query_given):
    factor = 1.0 / math.sqrt(HD)
    peak, total, summed = carry
    k_heads = head_major(k_rows)
    v_heads = head_major(v_rows)
    scores = (
        jnp.einsum("hqd,hkd->hqk", q_heads, k_heads, preferred_element_type=jnp.float32) * factor
    )
    allowed = (query_given[:, None] == 0) | (key_given[None, :] == 1)
    scores = jnp.where(allowed[None], scores, neg_fill)
    new_peak = jnp.maximum(peak, jnp.max(scores, axis=2))
    rescale = jnp.exp(peak - new_peak)
    weights = jnp.where(allowed[None], jnp.exp(scores - new_peak[..., None]), 0.0)
    total = total * rescale + jnp.sum(weights, axis=2)
    summed = summed * rescale[..., None] + jnp.einsum(
        "hqk,hkd->hqd", weights.astype(jnp.bfloat16), v_heads, preferred_element_type=jnp.float32
    )
    return (new_peak, total, summed)


def fresh_carry(heads_count, row_count):
    return (
        jnp.full((heads_count, row_count), neg_fill, jnp.float32),
        jnp.zeros((heads_count, row_count), jnp.float32),
        jnp.zeros((heads_count, row_count, HD), jnp.float32),
    )


def scan_keys(all_k, all_v, key_given, q_heads, query_given):
    key_count = all_k.shape[0]
    block = 512
    blocks = key_count // block
    k_blocks = all_k.reshape(blocks, block, all_k.shape[1])
    v_blocks = all_v.reshape(blocks, block, all_v.shape[1])
    g_blocks = key_given.reshape(blocks, block)

    def scan_step(carry, pieces):
        return (keyframe_step(carry, pieces[0], pieces[1], pieces[2], q_heads, query_given), None)

    start_carry = fresh_carry(q_heads.shape[0], q_heads.shape[1])
    result, unused = lax.scan(scan_step, start_carry, (k_blocks, v_blocks, g_blocks))
    return result


def body(
    global_q,
    global_k,
    global_v,
    keyframe_mask,
    global_wo,
    local_q,
    local_k,
    local_v,
    anchor_k,
    anchor_v,
):
    q_heads = head_major(global_q)
    query_rows = q_heads.shape[1]
    flags = keyframe_mask.astype(jnp.bfloat16)
    query_given = jnp.repeat(keyframe_mask, PG)
    all_k, all_v, all_flags = (
        lax.all_gather(global_k, "tm", axis=0, tiled=True),
        lax.all_gather(global_v, "tm", axis=0, tiled=True),
        lax.all_gather(flags, "tm", axis=0, tiled=True),
    )
    key_given = jnp.repeat(all_flags, PG)
    peak, total, summed = scan_keys(all_k, all_v, key_given, q_heads, query_given)
    attended = summed / total[..., None]
    attended = jnp.transpose(attended, (1, 0, 2)).reshape(query_rows, -1).astype(jnp.bfloat16)
    projected = jnp.dot(attended, global_wo, preferred_element_type=jnp.float32)
    global_out = lax.psum_scatter(
        projected.astype(jnp.bfloat16), "mp", scatter_dimension=1, tiled=True
    )
    stacked = jnp.stack([anchor_k, anchor_v])
    following = passed_along(stacked, "tm", -1)
    present = lax.axis_index("tm") < lax.axis_size("tm") - 1
    local_heads = head_major(local_q)
    own_k = jnp.concatenate([anchor_k, local_k], axis=0)
    own_v = jnp.concatenate([anchor_v, local_v], axis=0)
    anchor_rows = anchor_k.shape[0]
    every_k = jnp.concatenate([own_k, following[0]], axis=0)
    every_v = jnp.concatenate([own_v, following[1]], axis=0)
    valid = jnp.concatenate([jnp.ones((own_k.shape[0],), bool), jnp.full((anchor_rows,), present)])
    peak, total, summed = softmax_parts(
        local_heads, head_major(every_k), head_major(every_v), valid
    )
    local_result = summed / total[..., None]
    local_out = (
        jnp.transpose(local_result, (1, 0, 2)).reshape(local_q.shape[0], -1).astype(jnp.bfloat16)
    )
    return (global_out, local_out)


def solution(mesh):
    return jax.shard_map(
        body,
        mesh=mesh,
        in_specs=(
            P("tm", "mp"),
            P("tm", "mp"),
            P("tm", "mp"),
            P("tm"),
            P("mp", None),
            P("tm", "mp"),
            P("tm", "mp"),
            P("tm", "mp"),
            P("tm", "mp"),
            P("tm", "mp"),
        ),
        out_specs=(P("tm", "mp"), P("tm", "mp")),
        check_vma=False,
    )
```

profile of v0, /device:TPU:1, one launch (start us, length us, event | category | flops | bytes accessed | tf_op | source)
XLA Modules:
  0.0 547.1 jit_solution(16843142348087914347)
XLA Ops:
  9.7 5.1 collective-permute-start
  17.6 278.2 %all-reduce.1 = bf16[128]{0:T(256)(128)(2,1)S(1)} all-reduce(bf16[128]{0:T(256)(128)(2,1)S(1)} %dynamic-update-slice), channel_id=1, replica_groups=mesh['tm'=128,'mp'=2] {'tm'}, use_global_device_ids=true, to_apply=%add.1 | all-reduce | flops 128 | bytes 512
  297.6 2.3 copy.36
  301.5 1.9 copy.38
  304.1 6.4 %maximum_bitcast_fusion = bf16[8,1144,128]{2,0,1:T(8,128)(2,1)S(1)} fusion(bf16[88,8,128]{2,1,0:T(8,128)(2,1)S(1)} %bitcast.114, bf16[968,8,128]{2,1,0:T(8,128)(2,1)} %bitcast.105, bf16[88,8,128]{2,1,0:T(8,128)(2,1)S(1)} %bitcast.113), kind=kLoop, calls=%fused_computation.44 | loop fusion | flops 2342912 | bytes 4685824 | tf_op jit(solution)/shard_map/transpose | solution.py:22
  310.5 1.8 copy.28
  312.3 6.3 %maximum_bitcast_fusion.1 = bf16[8,1144,128]{2,0,1:T(8,128)(2,1)S(1)} fusion(bf16[88,8,128]{2,1,0:T(8,128)(2,1)S(1)} %bitcast.115, bf16[968,8,128]{2,1,0:T(8,128)(2,1)S(1)} %bitcast.104, bf16[88,8,128]{2,1,0:T(8,128)(2,1)S(1)} %bitcast.112), kind=kLoop, calls=%fused_computation.45 | loop fusion | flops 2342912 | bytes 4685824 | tf_op jit(solution)/shard_map/transpose | solution.py:22
  319.0 75.8 %while.27 = (s32[]{:T(128)}, f32[8,968]{1,0:T(8,128)S(1)}, f32[8,968,128]{2,1,0:T(8,128)}, pred[1144]{0:T(1024)(128)(4,1)S(1)}, bf16[8,968,128]{2,1,0:T(8,128)(2...) while((s32[]{:T(128)}, f32[8,968]{1,0:T(8,128)S(1)}, ...), condition=%wide.region_8.9_spmd, body=%wide.region_5.8_spmd.sunk | while | flops 576949312 | bytes 32397076 | solution.py:37
  319.0 2.1 fusion.61
  321.1 2.0 copy-done
  324.2 4.2 fusion.63
  328.4 2.1 fusion.61
  330.6 2.0 copy-done
  333.7 4.2 fusion.63
  337.9 2.1 fusion.61
  340.0 2.0 copy-done
  343.2 4.2 fusion.63
  347.4 2.1 fusion.61
  349.5 2.0 copy-done
  352.7 4.2 fusion.63
  356.9 2.1 fusion.61
  359.0 2.0 copy-done
  362.1 4.2 fusion.63
  366.4 2.1 fusion.61
  368.5 2.0 copy-done
  371.6 4.2 fusion.63
  375.8 2.1 fusion.61
  377.9 2.0 copy-done
  381.1 4.2 fusion.63
  385.3 2.1 fusion.61
  387.4 2.0 copy-done
  390.5 4.2 fusion.63
  394.8 58.6 %all-gather.5.cloned.1.call-done = bf16[4096,1024]{1,0:T(8,128)(2,1)} async-done(((bf16[32,1024]{1,0:T(8,128)(2,1)}), bf16[4096,1024]{1,0:T(8,128)(2,1)}) %all-gather.5.cloned.1.call-update) | async-done | bytes 8388624 | tf_op jit(solution)/shard_map/all_gather | solution.py:102
  453.4 67.6 %while.28 = (s32[]{:T(128)}, f32[8,32]{1,0:T(8,128)S(1)}, f32[8,32]{1,0:T(8,128)S(1)}, f32[8,32,128]{2,1,0:T(8,128)S(1)}, bf16[8,512]{1,0:T(8,128)(2,1)}, /*inde...) while((s32[]{:T(128)}, f32[8,32]{1,0:T(8,128)S(1)}, ...), condition=%wide.region_3.4_spmd.clone, body=%wide.region_0.3_spmd.clone.sunk | while | flops 68390144 | bytes 16601235 | solution.py:80
  453.4 1.7 constant_dynamic-slice_fusion.3
  456.4 1.6 copy.53
  461.8 1.7 constant_dynamic-slice_fusion.3
  464.8 1.6 copy.53
  470.2 1.7 constant_dynamic-slice_fusion.3
  473.3 1.6 copy.53
  478.7 1.7 constant_dynamic-slice_fusion.3
  487.1 1.7 constant_dynamic-slice_fusion.3
  495.6 1.7 constant_dynamic-slice_fusion.3
  504.0 1.7 constant_dynamic-slice_fusion.3
  512.5 1.7 constant_dynamic-slice_fusion.3
  520.9 3.7 convolution_convert_fusion
  524.7 3.7 copy_bitcast_fusion
  528.4 12.2 %reduce-scatter.2.cloned.1.call-done = bf16[32,1024]{1,0:T(8,128)(2,1)} async-done(((bf16[32,2048]{1,0:T(8,128)(2,1)}), bf16[32,1024]{1,0:T(8,128)(2,1)}) %reduce-scatter.2.cloned.1.call-update) | async-done | bytes 65552 | tf_op jit(solution)/shard_map/reduce_scatter | solution.py:110
  (161 shorter events, 61.2 us)
Async XLA Ops:
  7.2 387.6 %all-gather.3.cloned.1.call-start = ((), (), s32[]{:S(2)}) async-start(), calls=%async_computation.1 | async-start | bytes 8454144 | tf_op jit(solution)/shard_map/all_gather | solution.py:101
  7.9 445.5 %all-gather.5.cloned.1.call-start = ((), (), s32[]{:S(2)}) async-start(), calls=%async_computation.2 | async-start | bytes 8454144 | tf_op jit(solution)/shard_map/all_gather | solution.py:102
  8.6 531.9 %reduce-scatter.2.cloned.1.call-start = ((), (), s32[]{:S(2)}) async-start(), calls=%async_computation.3 | async-start | bytes 196608 | tf_op jit(solution)/shard_map/reduce_scatter | solution.py:110
  9.7 294.3 %collective-permute-start = (bf16[2,88,1024]{2,1,0:T(8,128)(2,1)S(1)}, bf16[2,88,1024]{2,1,0:T(8,128)(2,1)S(1)}, u32[]{:S(2)}, u32[]{:S(2)}) collective-permute-start(bf16[2,88,1024]{2,1,0:T(8,128)(2,1)S(1)} %pad_maximum_fusion), channel_id=1, source_target_pairs={{2,0},{4,2},{6,4},{8,6},{10,8},{12,10},{14,12},{16,14},{18,16},{20... | collective-permute-start | bytes 1081352 | tf_op jit(solution)/shard_map/ppermute | solution.py:18
  297.6 3.9 copy-start.1
  299.9 3.4 copy-start.3
  299.9 3.5 copy-start.2
  301.5 2.5 copy-start.4
  321.1 2.0 copy-start
  330.5 2.0 copy-start
  340.0 2.0 copy-start
  349.5 2.0 copy-start
  359.0 2.0 copy-start
  368.4 2.0 copy-start
  377.9 2.0 copy-start
  387.4 2.0 copy-start
  394.8 58.6 %copy-start.5 = (f32[8,968]{1,0:T(8,128)}, f32[8,968]{1,0:T(8,128)S(1)}, u32[]{:S(2)}) copy-start(f32[8,968]{1,0:T(8,128)S(1)} %get-tuple-element.91) | copy-start | bytes 92932
  520.9 3.8 copy-start.6
Sparse Core Ops, SparseCore 0:
  9.9 223.3 all-gather.2
  235.1 218.1 all-gather.4
  524.8 15.7 reduce-scatter.1
where the time goes:
time: 549 us; the launch traced here: 547 us
  blocking collectives  278 us (51%)
  local copies, waits for them, and re-layouts  76.2 us (14%)
  waiting for transfers between devices  72.1 us (13%)
  matrix products  61 us (11%)
  other arithmetic  33.6 us (6%)
  between operations  14.7 us (3%)
  loops' own time  6.02 us (1%)
    unnamed x1, blocking collectives  278 us
    all_gather x1, waiting for transfers between devices, body(): lax.all_gather(global_v, 'tm', axis=0, tiled=True)  58.6 us
    dot_general x8, matrix products, one_head(): jnp.dot(weights.astype(jnp.bfloat16), v_one, preferred_element_type=jnp.f...  33.7 us
    dynamic_slice x24, local copies, waits for them, and re-layouts, scan_keys(): lax.scan(scan_step, start_carry, (k_blocks, v_blocks, g_blocks))  28.7 us
    reshape x16, local copies, waits for them, and re-layouts, head_major(): return jnp.transpose(rows.reshape(rows.shape[0], -1, HD), (1, 0, 2))  18.2 us
    dot_general x8, matrix products, one_head(): jnp.einsum('qd,kd->qk', q_one, k_one, preferred_element_type=jnp.float32)  16.7 us
    while x24, local copies, waits for them, and re-layouts  16.2 us
    transpose x2, other arithmetic, head_major(): return jnp.transpose(rows.reshape(rows.shape[0], -1, HD), (1, 0, 2))  12.7 us
  transfers between devices with their start and end apart: 4, of which 2 were waited for; matrix products, arithmetic and copies ran while one was open for 16% of the time, Pallas kernels for 0%

commit v1 on v0

v1 whole, which is shorter than its diff:
```python
import math

import jax
import jax.numpy as jnp
from jax import lax
from jax.experimental import pallas as pl
from jax.experimental.pallas import tpu as pltpu
from jax.sharding import PartitionSpec as P

HD = 128
HEADS = 8
PG = 32
PL = 88
ROWS = 968
KEYS = 1152
FULL = 1024
CHUNKS = (240, 240, 240, 248)
FLAG = 16
BLOCK = PG * HEADS
MESH = pl.DeviceIdType.MESH
LOG2 = math.log2(math.e) / math.sqrt(HD)
LOW = -1e30
bf16, f32 = jnp.bfloat16, jnp.float32


def spread(parts):
    shape = (HD, HD)
    diagonal = lax.broadcasted_iota(jnp.int32, shape, 0) == lax.broadcasted_iota(jnp.int32, shape, 1)
    wide = [jnp.where(diagonal, jnp.broadcast_to(part, shape), 0.0).astype(bf16) for part in parts]
    ones = jnp.ones((len(parts) * HD, HD), bf16)
    return jnp.dot(jnp.concatenate(wide, axis=1), ones, preferred_element_type=f32)


def split_rows(wide):
    shape = (HD, HD)
    diagonal = lax.broadcasted_iota(jnp.int32, shape, 0) == lax.broadcasted_iota(jnp.int32, shape, 1)
    row = lax.broadcasted_iota(jnp.int32, (FLAG, HD), 0)
    tile = jnp.zeros((FLAG, HD), f32)
    blocks = wide.shape[0] // HD
    for block in range(blocks):
        rest = jnp.sum(jnp.where(diagonal, wide[block * HD : (block + 1) * HD], 0.0), axis=0, keepdims=True)
        for part in range(3):
            piece = rest.astype(bf16).astype(f32)
            tile = jnp.where(row == part * blocks + block, jnp.broadcast_to(piece, tile.shape), tile)
            rest = rest - piece
    return tile.astype(bf16)


def kernel(
    gq, gk, gv, mask, wo, lq, lk, lv, ak, av, gout, lout,
    gq_v, gk_v, gv_v, gsrc, grecv, qb, kvb, qcat, kcat, vcat, psend, precv, asend, arecv,
    wo_v, msend, mrecv, qv, kv, vv, akv, avv, nkv, nvv, ov, kf, va,
    in_sem, head_sem, out_sem, a_send, a_recv, q_send, q_recv, k_send, k_recv, p_send, p_recv,
    o_send, o_recv, m_send, m_recv, n_send, n_recv,
):
    t, mp = lax.axis_index("tm"), lax.axis_index("mp")
    y, xl, za, zb, c = t // 32, (t // 16) % 2, (t // 4) % 4, (t // 2) % 2, t % 2
    g = xl * 4 + zb * 2 + c

    def place(y, xl, za, zb, c):
        return y * 32 + xl * 16 + za * 4 + zb * 2 + c

    members = []
    for rel in range(1, 8):
        x2, z2, c2 = (xl + rel // 4) % 2, (zb + rel // 2 % 2) % 2, (c + rel % 2) % 2
        members.append((rel, x2 * 4 + z2 * 2 + c2, place(y, x2, za, z2, c2)))
    along_z = [(d, place(y, xl, (za + d) % 4, zb, c)) for d in (1, 2, 3)]
    along_y = [(d, place((y + d) % 4, xl, za, zb, c)) for d in (1, 2, 3)]
    before = (t + 127) % 128
    other = (t + 127 + 2 * c) % 128

    barrier = pltpu.get_barrier_semaphore()
    partners = [m[2] for m in members] + [p for _, p in along_z] + [p for _, p in along_y] + [other]
    for partner in partners:
        pl.semaphore_signal(barrier, inc=1, device_id={"tm": partner, "mp": mp}, device_id_type=MESH)
    pl.semaphore_signal(barrier, inc=1, device_id={"tm": t, "mp": 1 - mp}, device_id_type=MESH)

    def remote(src, dst, send, recv, partner):
        return pltpu.make_async_remote_copy(
            src_ref=src, dst_ref=dst, send_sem=send, recv_sem=recv,
            device_id={"tm": partner, "mp": mp}, device_id_type=MESH,
        )

    def head_columns(h):
        return pl.ds(h * HD, HD)

    own = [pltpu.make_async_copy(src, dst, in_sem.at[i]) for i, (src, dst) in enumerate(((gq, gq_v), (gk, gk_v), (gv, gv_v)))]
    wo_copy = pltpu.make_async_copy(wo, wo_v, in_sem.at[3])

    def head_copies(h):
        pairs = ((lq, qv), (lk, kv), (lv, vv), (ak, akv), (av, avv))
        return [
            pltpu.make_async_copy(src.at[:, head_columns(h)], dst.at[h], head_sem.at[i, h])
            for i, (src, dst) in enumerate(pairs)
        ]

    def out_copy(h):
        return pltpu.make_async_copy(ov.at[h], lout.at[:, head_columns(h)], out_sem.at[h])

    def anchor_copies(h):
        return [
            remote(src.at[:, head_columns(h)], dst.at[h], n_send.at[i, h], n_recv.at[i, h], before)
            for i, (src, dst) in enumerate(((ak, nkv), (av, nvv)))
        ]

    def member_copies():
        return [remote(gsrc.at[m], grecv.at[g], a_send.at[rel], a_recv.at[rel], p) for rel, m, p in members]

    def spread_copies():
        return [remote(qb.at[za], qb.at[za], q_send.at[d], q_recv.at[d], p) for d, p in along_z] + [
            remote(kvb.at[y], kvb.at[y], k_send.at[d], k_recv.at[d], p) for d, p in along_y
        ]

    def partial_copy(d, p):
        return remote(psend.at[d], precv.at[za], p_send.at[d], p_recv.at[d], p)

    def attended_copies():
        return [remote(asend.at[m], arecv.at[g], o_send.at[rel], o_recv.at[rel], p) for rel, m, p in members]

    for copy in own:
        copy.start()
    for copy in head_copies(0):
        copy.start()

    def start_head(h, unused):
        for copy in head_copies(h):
            copy.start()
        return unused

    lax.fori_loop(1, HEADS, start_head, 0)
    wo_copy.start()

    given = jnp.full((FLAG, 3 * HD), mask[0].astype(f32), f32).astype(bf16)
    for copy in own:
        copy.wait()
    for h in range(HEADS):
        columns = slice(h * HD, (h + 1) * HD)
        gsrc[h, :PG, :HD] = gq_v[:, columns]
        gsrc[h, :PG, HD : 2 * HD] = gk_v[:, columns]
        gsrc[h, :PG, 2 * HD :] = gv_v[:, columns]
        gsrc[h, PG:, :] = given
    grecv[g] = gsrc[g]
    va[:, HD:] = jnp.ones((KEYS, HD), bf16)
    vcat[:, HD:] = jnp.ones((4 * BLOCK, HD), bf16)

    pl.semaphore_wait(barrier, len(partners) + 1)
    for copy in member_copies():
        copy.start()

    def start_anchor(h, unused):
        for copy in anchor_copies(h):
            copy.start()
        return unused

    lax.fori_loop(0, HEADS, start_anchor, 0)

    def gather_blocks():
        for copy in member_copies():
            copy.wait_recv()
        row = lax.broadcasted_iota(jnp.int32, (FLAG, HD), 0)
        flags = jnp.zeros((FLAG, HD), f32)
        for m in range(HEADS):
            qb[za, m * PG : (m + 1) * PG, :] = grecv[m, :PG, :HD]
            kvb[y, m * PG : (m + 1) * PG, :] = grecv[m, :PG, HD:]
            flags = jnp.where(row == m, grecv[m, PG:, :HD].astype(f32), flags)
        flags = flags.astype(bf16)
        qb[za, BLOCK:, :] = flags
        kvb[y, BLOCK:, :HD] = flags
        kvb[y, BLOCK:, HD:] = flags
        for copy in spread_copies():
            copy.start()

    def keyframe_attention():
        for copy in spread_copies():
            copy.wait_recv()
        first = lax.broadcasted_iota(jnp.int32, (PG, HD), 1) == 0
        for s in range(4):
            rows = slice(s * BLOCK, (s + 1) * BLOCK)
            qcat[rows, :HD] = qb[s, :BLOCK, :]
            kcat[rows, :HD] = kvb[s, :BLOCK, :HD]
            vcat[rows, :HD] = kvb[s, :BLOCK, HD:]
            q_flags = qb[s, BLOCK:, :].astype(f32)
            k_flags = kvb[s, BLOCK:, :HD].astype(f32)
            for m in range(HEADS):
                part = slice(s * BLOCK + m * PG, s * BLOCK + (m + 1) * PG)
                q_flag = jnp.broadcast_to(q_flags[m : m + 1, :], (PG, HD))
                k_flag = jnp.broadcast_to(k_flags[m : m + 1, :], (PG, HD))
                qcat[part, HD:] = jnp.where(first, q_flag, 0.0).astype(bf16)
                kcat[part, HD:] = jnp.where(first, (k_flag - 1.0) * -LOW, 0.0).astype(bf16)
        for d in (2, 1, 3, 0):
            rows = pl.ds(pl.multiple_of((za + d) % 4 * BLOCK, BLOCK), BLOCK)
            scores = lax.dot_general(
                qcat[rows, :], kcat[...], (((1,), (1,)), ((), ())), preferred_element_type=f32
            )
            peak = jnp.max(scores, axis=1, keepdims=True)
            weights = jnp.exp2((scores - peak) * LOG2).astype(bf16)
            summed = jnp.dot(weights, vcat[...], preferred_element_type=f32)
            total = summed[:, HD:]
            mean = (summed[:, :HD] / total).astype(bf16)
            tile = split_rows(peak * LOG2 + jnp.log2(total))
            if d == 0:
                precv[za, :BLOCK, :] = mean
                precv[za, BLOCK:, :] = tile
            else:
                psend[d, :BLOCK, :] = mean
                psend[d, BLOCK:, :] = tile
                partial_copy(d, along_z[d - 1][1]).start()

    def combine_partials():
        for d, p in along_z:
            partial_copy(d, p).wait_recv()
        for block in range(BLOCK // HD):
            rows = slice(block * HD, (block + 1) * HD)
            logs = []
            for s in range(4):
                tile = precv[s, BLOCK:, :].astype(f32)
                logs.append(spread([tile[2 * part + block : 2 * part + block + 1, :] for part in range(3)]))
            peak = jnp.maximum(jnp.maximum(logs[0], logs[1]), jnp.maximum(logs[2], logs[3]))
            total = jnp.zeros((HD, HD), f32)
            summed = jnp.zeros((HD, HD), f32)
            for s in range(4):
                share = jnp.exp2(logs[s] - peak)
                total = total + share
                summed = summed + share * precv[s, rows, :].astype(f32)
            attended = (summed / total).astype(bf16)
            for m in range(HD // PG):
                asend[block * (HD // PG) + m] = attended[m * PG : (m + 1) * PG, :]
        arecv[g] = asend[g]
        for copy in attended_copies():
            copy.start()

    def project():
        for copy in attended_copies():
            copy.wait_recv()
        wo_copy.wait()
        attended = jnp.concatenate([arecv[h] for h in range(HEADS)], axis=1)
        half = HEADS * HD
        theirs = pl.ds(pl.multiple_of((1 - mp) * half, half), half)
        mine = pl.ds(pl.multiple_of(mp * half, half), half)
        msend[...] = jnp.dot(attended, wo_v[:, theirs], preferred_element_type=f32).astype(bf16)
        swap = pltpu.make_async_remote_copy(
            src_ref=msend, dst_ref=mrecv, send_sem=m_send, recv_sem=m_recv,
            device_id={"tm": t, "mp": 1 - mp}, device_id_type=MESH,
        )
        swap.start()
        kept = jnp.dot(attended, wo_v[:, mine], preferred_element_type=f32)
        swap.wait()
        gout[...] = (kept + mrecv[...].astype(f32)).astype(bf16)

    valid = jnp.where(t == 127, ROWS + PL, ROWS + 2 * PL) - FULL

    def local_scores(h, start, rows):
        q = (qv[h, start : start + rows, :].astype(f32) * LOG2).astype(bf16)
        scores = lax.dot_general(q, kf[...], (((1,), (1,)), ((), ())), preferred_element_type=f32)
        last = scores[:, FULL:]
        lane = lax.broadcasted_iota(jnp.int32, last.shape, 1)
        return jnp.concatenate([scores[:, :FULL], jnp.where(lane < valid, last, LOW)], axis=1)

    def local_head(h, unused):
        pl.when(h == 1)(gather_blocks)
        pl.when(h == 6)(keyframe_attention)
        for copy in head_copies(h):
            copy.wait()
        for copy in anchor_copies(h):
            copy.wait_recv()
        pad = jnp.zeros((KEYS - ROWS - 2 * PL, HD), f32)
        kf[...] = jnp.concatenate([x[h].astype(f32) for x in (kv, akv, nkv)] + [pad], axis=0).astype(bf16)
        va[:, :HD] = jnp.concatenate([x[h].astype(f32) for x in (vv, avv, nvv)] + [pad], axis=0).astype(bf16)
        starts = [sum(CHUNKS[:i]) for i in range(len(CHUNKS))]
        scores = local_scores(h, starts[0], CHUNKS[0])
        for i, (start, rows) in enumerate(zip(starts, CHUNKS)):
            now = scores
            if i + 1 < len(CHUNKS):
                scores = local_scores(h, starts[i + 1], CHUNKS[i + 1])
            peak = jnp.max(now, axis=1, keepdims=True)
            weights = jnp.exp2((now - peak).astype(bf16))
            summed = jnp.dot(weights, va[...], preferred_element_type=f32)
            ov[h, start : start + rows, :] = (summed[:, :HD] / summed[:, HD:]).astype(bf16)
        out_copy(h).start()
        return unused

    lax.fori_loop(0, HEADS, local_head, 0)
    combine_partials()
    project()

    def finish(h, unused):
        out_copy(h).wait()
        for copy in anchor_copies(h):
            copy.wait_send()
        return unused

    lax.fori_loop(0, HEADS, finish, 0)
    for copy in member_copies() + spread_copies() + [partial_copy(d, p) for d, p in along_z] + attended_copies():
        copy.wait_send()


def body(*args):
    dma = pltpu.SemaphoreType.DMA
    vmem = lambda *shape: pltpu.VMEM(shape, bf16)
    anywhere = pl.BlockSpec(memory_space=pl.ANY)
    width = HEADS * HD
    return pl.pallas_call(
        kernel,
        name="keyframe_and_infill",
        out_shape=(
            jax.ShapeDtypeStruct((PG, width), bf16),
            jax.ShapeDtypeStruct((ROWS, width), bf16),
        ),
        in_specs=[anywhere] * 3 + [pl.BlockSpec(memory_space=pltpu.SMEM)] + [anywhere] * 6,
        out_specs=(pl.BlockSpec(memory_space=pltpu.VMEM), anywhere),
        scratch_shapes=[
            vmem(PG, width), vmem(PG, width), vmem(PG, width),
            vmem(HEADS, PG + FLAG, 3 * HD), vmem(HEADS, PG + FLAG, 3 * HD),
            vmem(4, BLOCK + FLAG, HD), vmem(4, BLOCK + FLAG, 2 * HD),
            vmem(4 * BLOCK, 2 * HD), vmem(4 * BLOCK, 2 * HD), vmem(4 * BLOCK, 2 * HD),
            vmem(4, BLOCK + FLAG, HD), vmem(4, BLOCK + FLAG, HD),
            vmem(HEADS, PG, HD), vmem(HEADS, PG, HD),
            vmem(width, 2 * width), vmem(PG, width), vmem(PG, width),
            vmem(HEADS, ROWS, HD), vmem(HEADS, ROWS, HD), vmem(HEADS, ROWS, HD),
            vmem(HEADS, PL, HD), vmem(HEADS, PL, HD), vmem(HEADS, PL, HD), vmem(HEADS, PL, HD),
            vmem(HEADS, ROWS, HD), vmem(KEYS, HD), vmem(KEYS, 2 * HD),
            dma((4,)), dma((5, HEADS)), dma((HEADS,)),
            dma((8,)), dma((8,)), dma((4,)), dma((4,)), dma((4,)), dma((4,)), dma((4,)), dma((4,)),
            dma((8,)), dma((8,)), dma, dma, dma((2, HEADS)), dma((2, HEADS)),
        ],
        compiler_params=pltpu.CompilerParams(
            collective_id=1, has_side_effects=True, vmem_limit_bytes=60 * 2**20
        ),
    )(*args)


def solution(mesh):
    whole, rows = P("tm", "mp"), P("mp", None)
    return jax.shard_map(
        body,
        mesh=mesh,
        in_specs=(whole, whole, whole, P("tm"), rows) + (whole,) * 5,
        out_specs=(whole, whole),
        check_vma=False,
    )
```

time: 549 us -> 51.5 us (0.09)
  blocking collectives: 278 us -> 0 us
  waiting for transfers between devices: 72.1 us -> 0 us
  local copies, waits for them, and re-layouts: 76.2 us -> 4.46 us
  matrix products: 61 us -> 0 us
  Pallas kernels: 0 us -> 45.5 us
  other arithmetic: 33.6 us -> 0 us
  between operations: 14.7 us -> 1.29 us
  loops' own time: 6.02 us -> 0 us
    unnamed x1 -> x0, blocking collectives: 278 us -> none
    dot_general x33 -> x0, matrix products: 61 us -> none  [the longest x8 33.7 us: one_head(): jnp.dot(weights.astype(jnp.bfloat16), v_one, preferred_element_type=jnp.f...]
    all_gather x2 -> x0, waiting for transfers between devices: 58.6 us -> none  [the longest x1 58.6 us: body(): lax.all_gather(global_v, 'tm', axis=0, tiled=True)]
    pallas_call x0 -> x1, Pallas kernels: none -> 45.5 us  [body(): pl.pallas_call(kernel, name='keyframe_and_infill', out_shape=(jax.ShapeDt...]
    dynamic_slice x24 -> x0, local copies, waits for them, and re-layouts: 28.7 us -> none  [scan_keys(): lax.scan(scan_step, start_carry, (k_blocks, v_blocks, g_blocks))]
    while x27 -> x0, local copies, waits for them, and re-layouts: 19.8 us -> none
    reshape x16 -> x0, local copies, waits for them, and re-layouts: 18.2 us -> none  [head_major(): return jnp.transpose(rows.reshape(rows.shape[0], -1, HD), (1, 0, 2))]
    transpose x2 -> x0, other arithmetic: 12.7 us -> none  [head_major(): return jnp.transpose(rows.reshape(rows.shape[0], -1, HD), (1, 0, 2))]
  transfers between devices with their start and end apart: 4 -> 0, of which waited for: 2 -> 0; matrix products, arithmetic and copies ran while one was open for 16% -> 0% of each run, Pallas kernels for 0% -> 0%
where the time goes in v1:
time: 51.5 us; the launch traced here: 51.3 us
  Pallas kernels  45.5 us (88%)
  local copies, waits for them, and re-layouts  4.46 us (9%)
  between operations  1.29 us (3%)
    pallas_call x1, Pallas kernels, body(): pl.pallas_call(kernel, name='keyframe_and_infill', out_shape=(jax.ShapeDt...  45.5 us
    unnamed x2, local copies, waits for them, and re-layouts  4.46 us

profile of v1, /device:TPU:1, one launch (start us, length us, event | category | flops | bytes accessed | tf_op | source)
XLA Modules:
  0.0 51.3 jit_solution(416417998663399902)
XLA Ops:
  1.3 45.5 %keyframe_and_infill.1 = (bf16[32,1024]{1,0:T(8,128)(2,1)}, bf16[968,1024]{1,0:T(8,128)(2,1)}) custom-call(bf16[32,1024]{1,0:T(8,128)(2,1)} %gq.1, bf16[32,1024]{1,0:T(8,128)(2,1)} %gk.1, bf16[32,1024]{1,0:T(8,128)(2,1)} %gv.1, s32[1]{0:T(128)S(6)} %copy.14.mask, bf16[1024,2048]{1,0:T(8,128)(2,1)} %wo.1, bf16[968,1024]{1,0:T(8,128)(2,1)} %lq.1, ...), custom_call_target="tpu_custom_call" | custom-call | tf_op jit(solution)/shard_map/keyframe_and_infill/pallas_call | solution.py:302
  46.8 1.5 %copy.15 = bf16[32,1024]{1,0:T(8,128)(2,1)} copy(bf16[32,1024]{1,0:T(8,128)(2,1)} %get-tuple-element.4) | data formatting | bytes 131072
  48.3 3.0 %copy.16 = bf16[968,1024]{1,0:T(8,128)(2,1)} copy(bf16[968,1024]{1,0:T(8,128)(2,1)} %get-tuple-element.5) | data formatting | bytes 3964928

commit v2 on v1

--- a/solution.py
+++ b/solution.py
@@ -47,11 +47,10 @@
 
 
 def kernel(
-    gq, gk, gv, mask, wo, lq, lk, lv, ak, av, gout, lout,
-    gq_v, gk_v, gv_v, gsrc, grecv, qb, kvb, qcat, kcat, vcat, psend, precv, asend, arecv,
-    wo_v, msend, mrecv, qv, kv, vv, akv, avv, nkv, nvv, ov, kf, va,
+    gq, gk, gv, mask, wo, lq, lk, lv, ak, av, att, wo_other, wo_mine, lout,
+    gq_v, gk_v, gv_v, gsrc, grecv, qb, kvb, qcat, kcat, vcat, psend, precv, asend, qv, kv, vv, akv, avv, nkv, nvv, ov, kf, va,
     in_sem, head_sem, out_sem, a_send, a_recv, q_send, q_recv, k_send, k_recv, p_send, p_recv,
-    o_send, o_recv, m_send, m_recv, n_send, n_recv,
+    o_send, o_recv, w_send, w_recv, n_send, n_recv,
 ):
     t, mp = lax.axis_index("tm"), lax.axis_index("mp")
     y, xl, za, zb, c = t // 32, (t // 16) % 2, (t // 4) % 4, (t // 2) % 2, t % 2
@@ -60,10 +59,13 @@
     def place(y, xl, za, zb, c):
         return y * 32 + xl * 16 + za * 4 + zb * 2 + c
 
-    members = []
-    for rel in range(1, 8):
+    group = []
+    for rel in range(8):
         x2, z2, c2 = (xl + rel // 4) % 2, (zb + rel // 2 % 2) % 2, (c + rel % 2) % 2
-        members.append((rel, x2 * 4 + z2 * 2 + c2, place(y, x2, za, z2, c2)))
+        group.append((rel, x2 * 4 + z2 * 2 + c2, place(y, x2, za, z2, c2)))
+    members = group[1:]
+    across = place(y, 1 - xl, za, zb, c)
+    sibling = place(y, xl, za, zb, 1 - c)
     along_z = [(d, place(y, xl, (za + d) % 4, zb, c)) for d in (1, 2, 3)]
     along_y = [(d, place((y + d) % 4, xl, za, zb, c)) for d in (1, 2, 3)]
     before = (t + 127) % 128
@@ -71,21 +73,20 @@
 
     barrier = pltpu.get_barrier_semaphore()
     partners = [m[2] for m in members] + [p for _, p in along_z] + [p for _, p in along_y] + [other]
-    for partner in partners:
-        pl.semaphore_signal(barrier, inc=1, device_id={"tm": partner, "mp": mp}, device_id_type=MESH)
-    pl.semaphore_signal(barrier, inc=1, device_id={"tm": t, "mp": 1 - mp}, device_id_type=MESH)
-
-    def remote(src, dst, send, recv, partner):
+    partners = [(p, mp) for p in partners] + [(m[2], 1 - mp) for m in group]
+    for partner, side in partners:
+        pl.semaphore_signal(barrier, inc=1, device_id={"tm": partner, "mp": side}, device_id_type=MESH)
+
+    def remote(src, dst, send, recv, partner, side=mp):
         return pltpu.make_async_remote_copy(
             src_ref=src, dst_ref=dst, send_sem=send, recv_sem=recv,
-            device_id={"tm": partner, "mp": mp}, device_id_type=MESH,
+            device_id={"tm": partner, "mp": side}, device_id_type=MESH,
         )
 
     def head_columns(h):
         return pl.ds(h * HD, HD)
 
     own = [pltpu.make_async_copy(src, dst, in_sem.at[i]) for i, (src, dst) in enumerate(((gq, gq_v), (gk, gk_v), (gv, gv_v)))]
-    wo_copy = pltpu.make_async_copy(wo, wo_v, in_sem.at[3])
 
     def head_copies(h):
         pairs = ((lq, qv), (lk, kv), (lv, vv), (ak, akv), (av, avv))
@@ -95,7 +96,7 @@
         ]
 
     def out_copy(h):
-        return pltpu.make_async_copy(ov.at[h], lout.at[:, head_columns(h)], out_sem.at[h])
+        return pltpu.make_async_copy(ov.at[h], lout.at[h], out_sem.at[h])
 
     def anchor_copies(h):
         return [
@@ -115,7 +116,27 @@
         return remote(psend.at[d], precv.at[za], p_send.at[d], p_recv.at[d], p)
 
     def attended_copies():
-        return [remote(asend.at[m], arecv.at[g], o_send.at[rel], o_recv.at[rel], p) for rel, m, p in members]
+        slot = att.at[mp * HEADS + g]
+        return [
+            remote(asend.at[m], slot, o_send.at[rel + 8 * i], o_recv.at[rel + 8 * i], p, side)
+            for i, side in enumerate((mp, 1 - mp))
+            for rel, m, p in group[1 - i :]
+        ]
+
+    half = HEADS * HD
+    own_half = pl.ds(pl.multiple_of(c * (half // 2), half // 2), half // 2)
+
+    def wo_across():
+        src = wo.at[own_half, pl.ds(pl.multiple_of((1 - mp) * half, half), half)]
+        return remote(src, wo_other.at[own_half, :], w_send.at[0], w_recv.at[0], across, 1 - mp)
+
+    def wo_beside():
+        rows = wo_other.at[own_half, :]
+        return remote(rows, rows, w_send.at[1], w_recv.at[1], sibling)
+
+    mine = pl.ds(pl.multiple_of(mp * half, half), half)
+    wo_copy = pltpu.make_async_copy(wo.at[:, mine], wo_mine, in_sem.at[4])
+    own_slot = pltpu.make_async_copy(asend.at[g], att.at[mp * HEADS + g], in_sem.at[3])
 
     for copy in own:
         copy.start()
@@ -143,7 +164,7 @@
     va[:, HD:] = jnp.ones((KEYS, HD), bf16)
     vcat[:, HD:] = jnp.ones((4 * BLOCK, HD), bf16)
 
-    pl.semaphore_wait(barrier, len(partners) + 1)
+    pl.semaphore_wait(barrier, len(partners))
     for copy in member_copies():
         copy.start()
 
@@ -153,6 +174,7 @@
         return unused
 
     lax.fori_loop(0, HEADS, start_anchor, 0)
+    wo_across().start()
 
     def gather_blocks():
         for copy in member_copies():
@@ -225,27 +247,11 @@
             attended = (summed / total).astype(bf16)
             for m in range(HD // PG):
                 asend[block * (HD // PG) + m] = attended[m * PG : (m + 1) * PG, :]
-        arecv[g] = asend[g]
         for copy in attended_copies():
             copy.start()
-
-    def project():
-        for copy in attended_copies():
-            copy.wait_recv()
-        wo_copy.wait()
-        attended = jnp.concatenate([arecv[h] for h in range(HEADS)], axis=1)
-        half = HEADS * HD
-        theirs = pl.ds(pl.multiple_of((1 - mp) * half, half), half)
-        mine = pl.ds(pl.multiple_of(mp * half, half), half)
-        msend[...] = jnp.dot(attended, wo_v[:, theirs], preferred_element_type=f32).astype(bf16)
-        swap = pltpu.make_async_remote_copy(
-            src_ref=msend, dst_ref=mrecv, send_sem=m_send, recv_sem=m_recv,
-            device_id={"tm": t, "mp": 1 - mp}, device_id_type=MESH,
-        )
-        swap.start()
-        kept = jnp.dot(attended, wo_v[:, mine], preferred_element_type=f32)
-        swap.wait()
-        gout[...] = (kept + mrecv[...].astype(f32)).astype(bf16)
+        own_slot.start()
+        wo_across().wait_recv()
+        wo_beside().start()
 
     valid = jnp.where(t == 127, ROWS + PL, ROWS + 2 * PL) - FULL
 
@@ -257,8 +263,8 @@
         return jnp.concatenate([scores[:, :FULL], jnp.where(lane < valid, last, LOW)], axis=1)
 
     def local_head(h, unused):
-        pl.when(h == 1)(gather_blocks)
-        pl.when(h == 6)(keyframe_attention)
+        pl.when(h == 4)(keyframe_attention)
+        pl.when(h == 7)(combine_partials)
         for copy in head_copies(h):
             copy.wait()
         for copy in anchor_copies(h):
@@ -279,9 +285,8 @@
         out_copy(h).start()
         return unused
 
+    gather_blocks()
     lax.fori_loop(0, HEADS, local_head, 0)
-    combine_partials()
-    project()
 
     def finish(h, unused):
         out_copy(h).wait()
@@ -290,43 +295,72 @@
         return unused
 
     lax.fori_loop(0, HEADS, finish, 0)
-    for copy in member_copies() + spread_copies() + [partial_copy(d, p) for d, p in along_z] + attended_copies():
+    for copy in member_copies() + spread_copies() + [partial_copy(d, p) for d, p in along_z]:
         copy.wait_send()
+    for copy in attended_copies() + [wo_beside()]:
+        copy.wait()
+    wo_across().wait_send()
+    own_slot.wait()
+    wo_copy.wait()
+
+
+def project_kernel(att, wo_mine, wo_other, heads, gout, lout, out_sem):
+    mp = lax.axis_index("mp")
+    moves = [
+        pltpu.make_async_copy(heads.at[h], lout.at[:, pl.ds(h * HD, HD)], out_sem.at[h]) for h in range(HEADS)
+    ]
+    for move in moves:
+        move.start()
+    total = jnp.zeros(gout.shape, f32)
+    for side, wo in ((mp, wo_mine), (1 - mp, wo_other)):
+        attended = jnp.concatenate([att[side * HEADS + h] for h in range(HEADS)], axis=1)
+        total = total + jnp.dot(attended, wo[...], preferred_element_type=f32)
+    gout[...] = total.astype(bf16)
+    for move in moves:
+        move.wait()
 
 
 def body(*args):
     dma = pltpu.SemaphoreType.DMA
     vmem = lambda *shape: pltpu.VMEM(shape, bf16)
     anywhere = pl.BlockSpec(memory_space=pl.ANY)
+    in_vmem = pl.BlockSpec(memory_space=pltpu.VMEM)
     width = HEADS * HD
-    return pl.pallas_call(
+    att, wo_other, wo_mine, heads = pl.pallas_call(
         kernel,
         name="keyframe_and_infill",
-        out_shape=(
-            jax.ShapeDtypeStruct((PG, width), bf16),
-            jax.ShapeDtypeStruct((ROWS, width), bf16),
-        ),
+        out_shape=(vmem(2 * HEADS, PG, HD), vmem(width, width), vmem(width, width), vmem(HEADS, ROWS, HD)),
         in_specs=[anywhere] * 3 + [pl.BlockSpec(memory_space=pltpu.SMEM)] + [anywhere] * 6,
-        out_specs=(pl.BlockSpec(memory_space=pltpu.VMEM), anywhere),
+        out_specs=(anywhere,) * 4,
         scratch_shapes=[
             vmem(PG, width), vmem(PG, width), vmem(PG, width),
             vmem(HEADS, PG + FLAG, 3 * HD), vmem(HEADS, PG + FLAG, 3 * HD),
             vmem(4, BLOCK + FLAG, HD), vmem(4, BLOCK + FLAG, 2 * HD),
             vmem(4 * BLOCK, 2 * HD), vmem(4 * BLOCK, 2 * HD), vmem(4 * BLOCK, 2 * HD),
-            vmem(4, BLOCK + FLAG, HD), vmem(4, BLOCK + FLAG, HD),
-            vmem(HEADS, PG, HD), vmem(HEADS, PG, HD),
-            vmem(width, 2 * width), vmem(PG, width), vmem(PG, width),
+            vmem(4, BLOCK + FLAG, HD), vmem(4, BLOCK + FLAG, HD), vmem(HEADS, PG, HD),
             vmem(HEADS, ROWS, HD), vmem(HEADS, ROWS, HD), vmem(HEADS, ROWS, HD),
             vmem(HEADS, PL, HD), vmem(HEADS, PL, HD), vmem(HEADS, PL, HD), vmem(HEADS, PL, HD),
             vmem(HEADS, ROWS, HD), vmem(KEYS, HD), vmem(KEYS, 2 * HD),
-            dma((4,)), dma((5, HEADS)), dma((HEADS,)),
+            dma((5,)), dma((5, HEADS)), dma((HEADS,)),
             dma((8,)), dma((8,)), dma((4,)), dma((4,)), dma((4,)), dma((4,)), dma((4,)), dma((4,)),
-            dma((8,)), dma((8,)), dma, dma, dma((2, HEADS)), dma((2, HEADS)),
+            dma((16,)), dma((16,)), dma((2,)), dma((2,)), dma((2, HEADS)), dma((2, HEADS)),
         ],
         compiler_params=pltpu.CompilerParams(
-            collective_id=1, has_side_effects=True, vmem_limit_bytes=60 * 2**20
+            collective_id=1, has_side_effects=True, vmem_limit_bytes=44 * 2**20
         ),
-    )(*args)
+    )(*[arg if arg.ndim == 1 else pltpu.with_memory_space_constraint(arg, pltpu.HBM) for arg in args])
+    return pl.pallas_call(
+        project_kernel,
+        name="projection",
+        out_shape=(
+            jax.ShapeDtypeStruct((PG, width), bf16),
+            jax.ShapeDtypeStruct((ROWS, width), bf16),
+        ),
+        in_specs=[in_vmem] * 3 + [anywhere],
+        out_specs=(in_vmem, anywhere),
+        scratch_shapes=[dma((HEADS,))],
+        compiler_params=pltpu.CompilerParams(vmem_limit_bytes=8 * 2**20),
+    )(att, wo_mine, wo_other, heads)
 
 
 def solution(mesh):

time: 51.5 us -> 46 us (0.89)
  local copies, waits for them, and re-layouts: 4.46 us -> 0 us
  Pallas kernels: 45.5 us -> 44.6 us
    unnamed x2 -> x0, local copies, waits for them, and re-layouts: 4.46 us -> none
    pallas_call x1 -> x2, Pallas kernels: 45.5 us -> 44.6 us  [the longest x1 42.2 us: body(): pl.pallas_call(kernel, name='keyframe_and_infill', out_shape=(vmem(2 * HE...]
where the time goes in v2:
time: 46 us; the launch traced here: 45.9 us
  Pallas kernels  44.6 us (97%)
  between operations  1.29 us (3%)
    pallas_call x1, Pallas kernels, body(): pl.pallas_call(kernel, name='keyframe_and_infill', out_shape=(vmem(2 * HE...  42.2 us
    pallas_call x1, Pallas kernels, body(): pl.pallas_call(project_kernel, name='projection', out_shape=(jax.ShapeDty...  2.41 us

profile of v2, /device:TPU:1, one launch (start us, length us, event | category | flops | bytes accessed | tf_op | source)
XLA Modules:
  0.0 45.9 jit_solution(15220440775891936008)
XLA Ops:
  1.3 42.2 %keyframe_and_infill.1 = (bf16[16,32,128]{2,1,0:T(8,128)(2,1)S(1)}, bf16[1024,1024]{1,0:T(8,128)(2,1)S(1)}, bf16[1024,1024]{1,0:T(8,128)(2,1)S(1)}, bf16[8,968,128]{2,1,0:T(8,128)(2,1)S(1)}) custom-call(bf16[32,1024]{1,0:T(8,128)(2,1)} %gq.1, bf16[32,1024]{1,0:T(8,128)(2,1)} %gk.1, bf16[32,1024]{1,0:T(8,128)(2,1)} %gv.1, s32[1]{0:T(128)S(6)} %copy.12.mask, ...), custom_call_target="tpu_custom_call" | custom-call | tf_op jit(solution)/shard_map/keyframe_and_infill/pallas_call | solution.py:329
  43.5 2.4 %projection.1 = (bf16[32,1024]{1,0:T(8,128)(2,1)}, bf16[968,1024]{1,0:T(8,128)(2,1)}) custom-call(bf16[16,32,128]{2,1,0:T(8,128)(2,1)S(1)} %get-tuple-element.6.att, bf16[1024,1024]{1,0:T(8,128)(2,1)S(1)} %get-tuple-element.7.wo_mine, bf16[1024,1024]{1,0:T(8,128)(2,1)S(1)} %get-tuple-element.8.wo_other, bf16[8,968,128]{2,1,0:T(8,128)(2,1)S(1)} %get-tuple-element.9.heads), custom_call_target="tpu_custom_call" | custom-call | tf_op jit(solution)/shard_map/projection/pallas_call | solution.py:352

commit v3 on v2

--- a/solution.py
+++ b/solution.py
@@ -48,8 +48,8 @@
 
 def kernel(
     gq, gk, gv, mask, wo, lq, lk, lv, ak, av, att, wo_other, wo_mine, lout,
-    gq_v, gk_v, gv_v, gsrc, grecv, qb, kvb, qcat, kcat, vcat, psend, precv, asend, qv, kv, vv, akv, avv, nkv, nvv, ov, kf, va,
-    in_sem, head_sem, out_sem, a_send, a_recv, q_send, q_recv, k_send, k_recv, p_send, p_recv,
+    gq_v, gk_v, gv_v, gsrc, grecv, qb, kb, qcat, kcat, vcat, wcat, psend, precv, asend, qv, kv, vv, akv, avv, nkv, nvv, ov, kf, va,
+    in_sem, head_sem, out_sem, a_send, a_recv, q_send, q_recv, k_send, k_recv, v_send, v_recv, p_send, p_recv,
     o_send, o_recv, w_send, w_recv, n_send, n_recv,
 ):
     t, mp = lax.axis_index("tm"), lax.axis_index("mp")
@@ -71,9 +71,16 @@
     before = (t + 127) % 128
     other = (t + 127 + 2 * c) % 128
 
+    own = [
+        pltpu.make_async_copy(src, dst, in_sem.at[i])
+        for i, (src, dst) in enumerate(((gq, gq_v), (gk, gk_v), (gv, gv_v)))
+    ]
+    for copy in own:
+        copy.start()
+
     barrier = pltpu.get_barrier_semaphore()
-    partners = [m[2] for m in members] + [p for _, p in along_z] + [p for _, p in along_y] + [other]
-    partners = [(p, mp) for p in partners] + [(m[2], 1 - mp) for m in group]
+    partners = [(along_z[d][1], mp) for d in (1, 0, 2)] + [(along_y[d][1], mp) for d in (1, 0, 2)]
+    partners += [(m[2], mp) for m in members[::-1]] + [(other, mp)] + [(m[2], 1 - mp) for m in group]
     for partner, side in partners:
         pl.semaphore_signal(barrier, inc=1, device_id={"tm": partner, "mp": side}, device_id_type=MESH)
 
@@ -85,8 +92,6 @@
 
     def head_columns(h):
         return pl.ds(h * HD, HD)
-
-    own = [pltpu.make_async_copy(src, dst, in_sem.at[i]) for i, (src, dst) in enumerate(((gq, gq_v), (gk, gk_v), (gv, gv_v)))]
 
     def head_copies(h):
         pairs = ((lq, qv), (lk, kv), (lv, vv), (ak, akv), (av, avv))
@@ -96,7 +101,7 @@
         ]
 
     def out_copy(h):
-        return pltpu.make_async_copy(ov.at[h], lout.at[h], out_sem.at[h])
+        return pltpu.make_async_copy(ov.at[h], lout.at[:, head_columns(h)], out_sem.at[h])
 
     def anchor_copies(h):
         return [
@@ -107,10 +112,14 @@
     def member_copies():
         return [remote(gsrc.at[m], grecv.at[g], a_send.at[rel], a_recv.at[rel], p) for rel, m, p in members]
 
-    def spread_copies():
-        return [remote(qb.at[za], qb.at[za], q_send.at[d], q_recv.at[d], p) for d, p in along_z] + [
-            remote(kvb.at[y], kvb.at[y], k_send.at[d], k_recv.at[d], p) for d, p in along_y
+    def scores_copies():
+        return [remote(qb.at[za], qb.at[za], q_send.at[d], q_recv.at[d], along_z[d - 1][1]) for d in (2, 1, 3)] + [
+            remote(kb.at[y], kb.at[y], k_send.at[d], k_recv.at[d], along_y[d - 1][1]) for d in (2, 1, 3)
         ]
+
+    def values_copies():
+        rows = vcat.at[pl.ds(pl.multiple_of(y * BLOCK, BLOCK), BLOCK), :HD]
+        return [remote(rows, rows, v_send.at[d], v_recv.at[d], along_y[d - 1][1]) for d in (2, 1, 3)]
 
     def partial_copy(d, p):
         return remote(psend.at[d], precv.at[za], p_send.at[d], p_recv.at[d], p)
@@ -119,8 +128,8 @@
         slot = att.at[mp * HEADS + g]
         return [
             remote(asend.at[m], slot, o_send.at[rel + 8 * i], o_recv.at[rel + 8 * i], p, side)
-            for i, side in enumerate((mp, 1 - mp))
-            for rel, m, p in group[1 - i :]
+            for i, side in ((1, 1 - mp), (0, mp))
+            for rel, m, p in members[::-1] + group[:i]
         ]
 
     half = HEADS * HD
@@ -135,46 +144,33 @@
         return remote(rows, rows, w_send.at[1], w_recv.at[1], sibling)
 
     mine = pl.ds(pl.multiple_of(mp * half, half), half)
-    wo_copy = pltpu.make_async_copy(wo.at[:, mine], wo_mine, in_sem.at[4])
-    own_slot = pltpu.make_async_copy(asend.at[g], att.at[mp * HEADS + g], in_sem.at[3])
+    wo_copy = pltpu.make_async_copy(wo.at[:, mine], wo_mine, in_sem.at[5])
+    own_slot = pltpu.make_async_copy(asend.at[g], att.at[mp * HEADS + g], in_sem.at[4])
 
     for copy in own:
+        copy.wait()
+    given = jnp.full((FLAG, HD), mask[0].astype(f32), f32).astype(bf16)
+    for h in range(HEADS):
+        columns = slice(h * HD, (h + 1) * HD)
+        gsrc[h, :PG, :] = gq_v[:, columns]
+        gsrc[h, PG : 2 * PG, :] = gk_v[:, columns]
+        gsrc[h, 2 * PG : 3 * PG, :] = gv_v[:, columns]
+        gsrc[h, 3 * PG :, :] = given
+    pl.semaphore_wait(barrier, len(partners))
+    for copy in member_copies()[::-1]:
         copy.start()
-    for copy in head_copies(0):
-        copy.start()
 
     def start_head(h, unused):
-        for copy in head_copies(h):
+        for copy in anchor_copies(h) + head_copies(h):
             copy.start()
         return unused
 
-    lax.fori_loop(1, HEADS, start_head, 0)
+    lax.fori_loop(0, HEADS, start_head, 0)
+    wo_across().start()
     wo_copy.start()
-
-    given = jnp.full((FLAG, 3 * HD), mask[0].astype(f32), f32).astype(bf16)
-    for copy in own:
-        copy.wait()
-    for h in range(HEADS):
-        columns = slice(h * HD, (h + 1) * HD)
-        gsrc[h, :PG, :HD] = gq_v[:, columns]
-        gsrc[h, :PG, HD : 2 * HD] = gk_v[:, columns]
-        gsrc[h, :PG, 2 * HD :] = gv_v[:, columns]
-        gsrc[h, PG:, :] = given
     grecv[g] = gsrc[g]
     va[:, HD:] = jnp.ones((KEYS, HD), bf16)
     vcat[:, HD:] = jnp.ones((4 * BLOCK, HD), bf16)
-
-    pl.semaphore_wait(barrier, len(partners))
-    for copy in member_copies():
-        copy.start()
-
-    def start_anchor(h, unused):
-        for copy in anchor_copies(h):
-            copy.start()
-        return unused
-
-    lax.fori_loop(0, HEADS, start_anchor, 0)
-    wo_across().start()
 
     def gather_blocks():
         for copy in member_copies():
@@ -182,44 +178,47 @@
         row = lax.broadcasted_iota(jnp.int32, (FLAG, HD), 0)
         flags = jnp.zeros((FLAG, HD), f32)
         for m in range(HEADS):
-            qb[za, m * PG : (m + 1) * PG, :] = grecv[m, :PG, :HD]
-            kvb[y, m * PG : (m + 1) * PG, :] = grecv[m, :PG, HD:]
-            flags = jnp.where(row == m, grecv[m, PG:, :HD].astype(f32), flags)
-        flags = flags.astype(bf16)
-        qb[za, BLOCK:, :] = flags
-        kvb[y, BLOCK:, :HD] = flags
-        kvb[y, BLOCK:, HD:] = flags
-        for copy in spread_copies():
+            rows = slice(m * PG, (m + 1) * PG)
+            qb[za, rows, :] = grecv[m, :PG, :]
+            kb[y, rows, :] = grecv[m, PG : 2 * PG, :]
+            vcat[pl.ds(pl.multiple_of(y * BLOCK + m * PG, PG), PG), :HD] = grecv[m, 2 * PG : 3 * PG, :]
+            flags = jnp.where(row == m, grecv[m, 3 * PG :, :].astype(f32), flags)
+        qb[za, BLOCK:, :] = flags.astype(bf16)
+        kb[y, BLOCK:, :] = flags.astype(bf16)
+        for copy in scores_copies() + values_copies():
             copy.start()
 
     def keyframe_attention():
-        for copy in spread_copies():
+        for copy in scores_copies():
             copy.wait_recv()
         first = lax.broadcasted_iota(jnp.int32, (PG, HD), 1) == 0
         for s in range(4):
             rows = slice(s * BLOCK, (s + 1) * BLOCK)
             qcat[rows, :HD] = qb[s, :BLOCK, :]
-            kcat[rows, :HD] = kvb[s, :BLOCK, :HD]
-            vcat[rows, :HD] = kvb[s, :BLOCK, HD:]
+            kcat[rows, :HD] = kb[s, :BLOCK, :]
             q_flags = qb[s, BLOCK:, :].astype(f32)
-            k_flags = kvb[s, BLOCK:, :HD].astype(f32)
+            k_flags = kb[s, BLOCK:, :].astype(f32)
             for m in range(HEADS):
                 part = slice(s * BLOCK + m * PG, s * BLOCK + (m + 1) * PG)
                 q_flag = jnp.broadcast_to(q_flags[m : m + 1, :], (PG, HD))
                 k_flag = jnp.broadcast_to(k_flags[m : m + 1, :], (PG, HD))
                 qcat[part, HD:] = jnp.where(first, q_flag, 0.0).astype(bf16)
                 kcat[part, HD:] = jnp.where(first, (k_flag - 1.0) * -LOW, 0.0).astype(bf16)
+        peaks = {}
         for d in (2, 1, 3, 0):
             rows = pl.ds(pl.multiple_of((za + d) % 4 * BLOCK, BLOCK), BLOCK)
             scores = lax.dot_general(
                 qcat[rows, :], kcat[...], (((1,), (1,)), ((), ())), preferred_element_type=f32
             )
-            peak = jnp.max(scores, axis=1, keepdims=True)
-            weights = jnp.exp2((scores - peak) * LOG2).astype(bf16)
-            summed = jnp.dot(weights, vcat[...], preferred_element_type=f32)
+            peaks[d] = jnp.max(scores, axis=1, keepdims=True)
+            wcat[d] = jnp.exp2((scores - peaks[d]) * LOG2).astype(bf16)
+        for copy in values_copies():
+            copy.wait_recv()
+        for d in (2, 1, 3, 0):
+            summed = jnp.dot(wcat[d], vcat[...], preferred_element_type=f32)
             total = summed[:, HD:]
             mean = (summed[:, :HD] / total).astype(bf16)
-            tile = split_rows(peak * LOG2 + jnp.log2(total))
+            tile = split_rows(peaks[d] * LOG2 + jnp.log2(total))
             if d == 0:
                 precv[za, :BLOCK, :] = mean
                 precv[za, BLOCK:, :] = tile
@@ -295,7 +294,7 @@
         return unused
 
     lax.fori_loop(0, HEADS, finish, 0)
-    for copy in member_copies() + spread_copies() + [partial_copy(d, p) for d, p in along_z]:
+    for copy in member_copies() + scores_copies() + values_copies() + [partial_copy(d, p) for d, p in along_z]:
         copy.wait_send()
     for copy in attended_copies() + [wo_beside()]:
         copy.wait()
@@ -304,20 +303,16 @@
     wo_copy.wait()
 
 
-def project_kernel(att, wo_mine, wo_other, heads, gout, lout, out_sem):
+def project_kernel(att, wo_mine, wo_other, rows, gout, lout, out_sem):
     mp = lax.axis_index("mp")
-    moves = [
-        pltpu.make_async_copy(heads.at[h], lout.at[:, pl.ds(h * HD, HD)], out_sem.at[h]) for h in range(HEADS)
-    ]
-    for move in moves:
-        move.start()
+    move = pltpu.make_async_copy(rows, lout, out_sem)
+    move.start()
     total = jnp.zeros(gout.shape, f32)
     for side, wo in ((mp, wo_mine), (1 - mp, wo_other)):
         attended = jnp.concatenate([att[side * HEADS + h] for h in range(HEADS)], axis=1)
         total = total + jnp.dot(attended, wo[...], preferred_element_type=f32)
     gout[...] = total.astype(bf16)
-    for move in moves:
-        move.wait()
+    move.wait()
 
 
 def body(*args):
@@ -326,23 +321,23 @@
     anywhere = pl.BlockSpec(memory_space=pl.ANY)
     in_vmem = pl.BlockSpec(memory_space=pltpu.VMEM)
     width = HEADS * HD
-    att, wo_other, wo_mine, heads = pl.pallas_call(
+    att, wo_other, wo_mine, rows = pl.pallas_call(
         kernel,
         name="keyframe_and_infill",
-        out_shape=(vmem(2 * HEADS, PG, HD), vmem(width, width), vmem(width, width), vmem(HEADS, ROWS, HD)),
+        out_shape=(vmem(2 * HEADS, PG, HD), vmem(width, width), vmem(width, width), vmem(ROWS, width)),
         in_specs=[anywhere] * 3 + [pl.BlockSpec(memory_space=pltpu.SMEM)] + [anywhere] * 6,
         out_specs=(anywhere,) * 4,
         scratch_shapes=[
             vmem(PG, width), vmem(PG, width), vmem(PG, width),
-            vmem(HEADS, PG + FLAG, 3 * HD), vmem(HEADS, PG + FLAG, 3 * HD),
-            vmem(4, BLOCK + FLAG, HD), vmem(4, BLOCK + FLAG, 2 * HD),
-            vmem(4 * BLOCK, 2 * HD), vmem(4 * BLOCK, 2 * HD), vmem(4 * BLOCK, 2 * HD),
+            vmem(HEADS, 3 * PG + FLAG, HD), vmem(HEADS, 3 * PG + FLAG, HD),
+            vmem(4, BLOCK + FLAG, HD), vmem(4, BLOCK + FLAG, HD),
+            vmem(4 * BLOCK, 2 * HD), vmem(4 * BLOCK, 2 * HD), vmem(4 * BLOCK, 2 * HD), vmem(4, BLOCK, 4 * BLOCK),
             vmem(4, BLOCK + FLAG, HD), vmem(4, BLOCK + FLAG, HD), vmem(HEADS, PG, HD),
             vmem(HEADS, ROWS, HD), vmem(HEADS, ROWS, HD), vmem(HEADS, ROWS, HD),
             vmem(HEADS, PL, HD), vmem(HEADS, PL, HD), vmem(HEADS, PL, HD), vmem(HEADS, PL, HD),
             vmem(HEADS, ROWS, HD), vmem(KEYS, HD), vmem(KEYS, 2 * HD),
-            dma((5,)), dma((5, HEADS)), dma((HEADS,)),
-            dma((8,)), dma((8,)), dma((4,)), dma((4,)), dma((4,)), dma((4,)), dma((4,)), dma((4,)),
+            dma((6,)), dma((5, HEADS)), dma((HEADS,)),
+            dma((8,)), dma((8,)), dma((4,)), dma((4,)), dma((4,)), dma((4,)), dma((4,)), dma((4,)), dma((4,)), dma((4,)),
             dma((16,)), dma((16,)), dma((2,)), dma((2,)), dma((2, HEADS)), dma((2, HEADS)),
         ],
         compiler_params=pltpu.CompilerParams(
@@ -358,9 +353,9 @@
         ),
         in_specs=[in_vmem] * 3 + [anywhere],
         out_specs=(in_vmem, anywhere),
-        scratch_shapes=[dma((HEADS,))],
+        scratch_shapes=[dma],
         compiler_params=pltpu.CompilerParams(vmem_limit_bytes=8 * 2**20),
-    )(att, wo_mine, wo_other, heads)
+    )(att, wo_mine, wo_other, rows)
 
 
 def solution(mesh):

time: 46 us -> 42.4 us (0.922)
  Pallas kernels: 44.6 us -> 41 us
    pallas_call x1, Pallas kernels: 42.2 us -> 39 us  [body(): pl.pallas_call(kernel, name='keyframe_and_infill', out_shape=(vmem(2 * HE...]
where the time goes in v3:
time: 42.4 us; the launch traced here: 42.3 us
  Pallas kernels  41 us (97%)
  between operations  1.29 us (3%)
    pallas_call x1, Pallas kernels, body(): pl.pallas_call(kernel, name='keyframe_and_infill', out_shape=(vmem(2 * HE...  39 us
    pallas_call x1, Pallas kernels, body(): pl.pallas_call(project_kernel, name='projection', out_shape=(jax.ShapeDty...  1.96 us

profile of v3, /device:TPU:1, one launch (start us, length us, event | category | flops | bytes accessed | tf_op | source)
XLA Modules:
  0.0 42.3 jit_solution(1462274369132608755)
XLA Ops:
  1.3 39.0 %keyframe_and_infill.1 = (bf16[16,32,128]{2,1,0:T(8,128)(2,1)S(1)}, bf16[1024,1024]{1,0:T(8,128)(2,1)S(1)}, bf16[1024,1024]{1,0:T(8,128)(2,1)S(1)}, bf16[968,1024]{1,0:T(8,128)(2,1)S(1)}) custom-call(bf16[32,1024]{1,0:T(8,128)(2,1)} %gq.1, bf16[32,1024]{1,0:T(8,128)(2,1)} %gk.1, bf16[32,1024]{1,0:T(8,128)(2,1)} %gv.1, s32[1]{0:T(128)S(6)} %copy.12.mask, ...), custom_call_target="tpu_custom_call" | custom-call | tf_op jit(solution)/shard_map/keyframe_and_infill/pallas_call | solution.py:324
  40.3 2.0 %projection.1 = (bf16[32,1024]{1,0:T(8,128)(2,1)}, bf16[968,1024]{1,0:T(8,128)(2,1)}) custom-call(bf16[16,32,128]{2,1,0:T(8,128)(2,1)S(1)} %get-tuple-element.6.att, bf16[1024,1024]{1,0:T(8,128)(2,1)S(1)} %get-tuple-element.7.wo_mine, bf16[1024,1024]{1,0:T(8,128)(2,1)S(1)} %get-tuple-element.8.wo_other, bf16[968,1024]{1,0:T(8,128)(2,1)S(1)} %get-tuple-element.9.rows), custom_call_target="tpu_custom_call" | custom-call | tf_op jit(solution)/shard_map/projection/pallas_call | solution.py:347

commit v4 on v3

--- a/solution.py
+++ b/solution.py
@@ -48,7 +48,7 @@
 
 def kernel(
     gq, gk, gv, mask, wo, lq, lk, lv, ak, av, att, wo_other, wo_mine, lout,
-    gq_v, gk_v, gv_v, gsrc, grecv, qb, kb, qcat, kcat, vcat, wcat, psend, precv, asend, qv, kv, vv, akv, avv, nkv, nvv, ov, kf, va,
+    gq_v, gk_v, gv_v, gsrc, grecv, qb, kb, qcat, kcat, vcat, psend, precv, asend, qv, kv, vv, akv, avv, nkv, nvv, ov, kf, va,
     in_sem, head_sem, out_sem, a_send, a_recv, q_send, q_recv, k_send, k_recv, v_send, v_recv, p_send, p_recv,
     o_send, o_recv, w_send, w_recv, n_send, n_recv,
 ):
@@ -204,21 +204,19 @@
                 k_flag = jnp.broadcast_to(k_flags[m : m + 1, :], (PG, HD))
                 qcat[part, HD:] = jnp.where(first, q_flag, 0.0).astype(bf16)
                 kcat[part, HD:] = jnp.where(first, (k_flag - 1.0) * -LOW, 0.0).astype(bf16)
-        peaks = {}
+        for copy in values_copies():
+            copy.wait_recv()
         for d in (2, 1, 3, 0):
             rows = pl.ds(pl.multiple_of((za + d) % 4 * BLOCK, BLOCK), BLOCK)
             scores = lax.dot_general(
                 qcat[rows, :], kcat[...], (((1,), (1,)), ((), ())), preferred_element_type=f32
             )
-            peaks[d] = jnp.max(scores, axis=1, keepdims=True)
-            wcat[d] = jnp.exp2((scores - peaks[d]) * LOG2).astype(bf16)
-        for copy in values_copies():
-            copy.wait_recv()
-        for d in (2, 1, 3, 0):
-            summed = jnp.dot(wcat[d], vcat[...], preferred_element_type=f32)
+            peak = jnp.max(scores, axis=1, keepdims=True)
+            weights = jnp.exp2((scores - peak) * LOG2).astype(bf16)
+            summed = jnp.dot(weights, vcat[...], preferred_element_type=f32)
             total = summed[:, HD:]
             mean = (summed[:, :HD] / total).astype(bf16)
-            tile = split_rows(peaks[d] * LOG2 + jnp.log2(total))
+            tile = split_rows(peak * LOG2 + jnp.log2(total))
             if d == 0:
                 precv[za, :BLOCK, :] = mean
                 precv[za, BLOCK:, :] = tile
@@ -331,7 +329,7 @@
             vmem(PG, width), vmem(PG, width), vmem(PG, width),
             vmem(HEADS, 3 * PG + FLAG, HD), vmem(HEADS, 3 * PG + FLAG, HD),
             vmem(4, BLOCK + FLAG, HD), vmem(4, BLOCK + FLAG, HD),
-            vmem(4 * BLOCK, 2 * HD), vmem(4 * BLOCK, 2 * HD), vmem(4 * BLOCK, 2 * HD), vmem(4, BLOCK, 4 * BLOCK),
+            vmem(4 * BLOCK, 2 * HD), vmem(4 * BLOCK, 2 * HD), vmem(4 * BLOCK, 2 * HD),
             vmem(4, BLOCK + FLAG, HD), vmem(4, BLOCK + FLAG, HD), vmem(HEADS, PG, HD),
             vmem(HEADS, ROWS, HD), vmem(HEADS, ROWS, HD), vmem(HEADS, ROWS, HD),
             vmem(HEADS, PL, HD), vmem(HEADS, PL, HD), vmem(HEADS, PL, HD), vmem(HEADS, PL, HD),

time: 42.4 us -> 43 us (1.014)
  Pallas kernels: 41 us -> 41.6 us
    pallas_call x1, Pallas kernels: 39 us -> 39.6 us  [body(): pl.pallas_call(kernel, name='keyframe_and_infill', out_shape=(vmem(2 * HE...]
where the time goes in v4:
time: 43 us; the launch traced here: 42.9 us
  Pallas kernels  41.6 us (97%)
  between operations  1.29 us (3%)
    pallas_call x1, Pallas kernels, body(): pl.pallas_call(kernel, name='keyframe_and_infill', out_shape=(vmem(2 * HE...  39.6 us
    pallas_call x1, Pallas kernels, body(): pl.pallas_call(project_kernel, name='projection', out_shape=(jax.ShapeDty...  1.96 us

profile of v4, /device:TPU:1, one launch (start us, length us, event | category | flops | bytes accessed | tf_op | source)
XLA Modules:
  0.0 42.9 jit_solution(1037717564612172238)
XLA Ops:
  1.3 39.6 %keyframe_and_infill.1 = (bf16[16,32,128]{2,1,0:T(8,128)(2,1)S(1)}, bf16[1024,1024]{1,0:T(8,128)(2,1)S(1)}, bf16[1024,1024]{1,0:T(8,128)(2,1)S(1)}, bf16[968,1024]{1,0:T(8,128)(2,1)S(1)}) custom-call(bf16[32,1024]{1,0:T(8,128)(2,1)} %gq.1, bf16[32,1024]{1,0:T(8,128)(2,1)} %gk.1, bf16[32,1024]{1,0:T(8,128)(2,1)} %gv.1, s32[1]{0:T(128)S(6)} %copy.12.mask, ...), custom_call_target="tpu_custom_call" | custom-call | tf_op jit(solution)/shard_map/keyframe_and_infill/pallas_call | solution.py:322
  40.9 2.0 %projection.1 = (bf16[32,1024]{1,0:T(8,128)(2,1)}, bf16[968,1024]{1,0:T(8,128)(2,1)}) custom-call(bf16[16,32,128]{2,1,0:T(8,128)(2,1)S(1)} %get-tuple-element.6.att, bf16[1024,1024]{1,0:T(8,128)(2,1)S(1)} %get-tuple-element.7.wo_mine, bf16[1024,1024]{1,0:T(8,128)(2,1)S(1)} %get-tuple-element.8.wo_other, bf16[968,1024]{1,0:T(8,128)(2,1)S(1)} %get-tuple-element.9.rows), custom_call_target="tpu_custom_call" | custom-call | tf_op jit(solution)/shard_map/projection/pallas_call | solution.py:345
